TPU v7x, 32 devices: a whole 2x2x4 slice. The times are simulated.
32 devices in a mesh: groups: 2 (over y), ctx: 16 (over z, x, core).
Axes of the slice: x: 2, y: 2, z: 4, core: 2. Of those that a mesh axis runs over, the one named last changes fastest.
Arguments:
- queries: bfloat16 [512, 6144], P(('groups', 'ctx')), parts along dimension 0, may hold values from -8 to 8
- latents: bfloat16 [4096, 576], P(('groups', 'ctx')), parts along dimension 0, may hold values from -8 to 8
- w_uk: bfloat16 [32, 128, 512], replicated, may hold values from -0.5 to 0.5
- w_uv: bfloat16 [32, 512, 128], replicated, may hold values from -1.5 to 1.5
Outputs:
- attended: bfloat16 [512, 4096], P(('groups', 'ctx')), parts along dimension 0
There are 2 independent parts, one for each index of `groups`. A program takes and returns all parts, laid end to end along the dimension named above; an argument that names none is the same for every part. Nothing has to cross between parts.
All inputs are finite; a program needn't handle non-finite values.
Results may differ from a plain program's by a relative error of at most 0.008.
Values may be sent and summed in bfloat16 or wider, within the bound.
A program may use at most 128 MiB of HBM per device.

v0:
```python
import math

import jax
import jax.numpy as jnp
from jax import lax
from jax.sharding import PartitionSpec as P

NOPE = 128
ROPE = 64
RANK = 512
VDIM = 128


def body(queries, latents, w_uk, w_uv):
    index = lax.axis_index("ctx")
    qrows = queries.shape[0]
    krows = latents.shape[0]
    offset = krows - qrows
    heads = w_uk.shape[0]
    query_pos = index * krows + offset + jnp.arange(qrows, dtype=jnp.int32)
    shaped = queries.reshape(qrows, heads, NOPE + ROPE)
    q_lat = jnp.einsum(
        "thi,hil->thl", shaped[:, :, :NOPE], w_uk, preferred_element_type=jnp.float32
    ).astype(jnp.bfloat16)
    q_rope = shaped[:, :, NOPE:]
    scale = 1.0 / jnp.sqrt(jnp.float32(NOPE + ROPE))
    last_query = jnp.max(query_pos)

    def inner(state, block, kstart):
        sub = block.shape[0]
        kpos = kstart + jnp.arange(sub, dtype=jnp.int32)

        def work(carried):
            running, total, acc = carried
            score = jnp.einsum(
                "thl,jl->thj", q_lat, block[:, :RANK], preferred_element_type=jnp.float32
            )
            score = score + jnp.einsum(
                "thr,jr->thj", q_rope, block[:, RANK:], preferred_element_type=jnp.float32
            )
            score = score * scale
            allowed = kpos[None, None, :] <= query_pos[:, None, None]
            score = jnp.where(allowed, score, -jnp.inf)
            fresh = jnp.maximum(running, jnp.max(score, axis=-1))
            expo = jnp.exp(score - fresh[:, :, None])
            factor = jnp.exp(running - fresh)
            total = total * factor + jnp.sum(expo, axis=-1)
            acc = acc * factor[:, :, None] + jnp.einsum(
                "thj,jl->thl",
                expo.astype(jnp.bfloat16),
                block[:, :RANK],
                preferred_element_type=jnp.float32,
            )
            return (fresh, total, acc)

        return lax.cond(kstart > last_query, lambda carried: carried, work, state)

    def accumulate(carry, piece, start):
        count = piece.shape[0]
        sub = math.gcd(count, 2048)
        if sub == count:
            return inner(carry, piece, start)
        blocks = piece.reshape(count // sub, sub, piece.shape[1])
        starts = start + jnp.arange(count // sub, dtype=jnp.int32) * sub

        def step(state, items):
            return (inner(state, items[0], items[1]), None)

        result, unused = lax.scan(step, carry, (blocks, starts))
        return result

    init = (
        jnp.full((qrows, heads), -1e30, jnp.float32),
        jnp.zeros((qrows, heads), jnp.float32),
        jnp.zeros((qrows, heads, RANK), jnp.float32),
    )
    running, total, acc = accumulate(
        init, lax.all_gather(latents, "ctx", axis=0, tiled=True), jnp.int32(0)
    )
    o_lat = (acc / total[:, :, None]).astype(jnp.bfloat16)
    result = jnp.einsum("thl,hlc->thc", o_lat, w_uv, preferred_element_type=jnp.float32).astype(
        jnp.bfloat16
    )
    result = result.reshape(qrows, heads * VDIM)
    return result


def solution(mesh):
    placed = (P(("groups", "ctx"), None), P(("groups", "ctx"), None), P(), P())
    return jax.shard_map(
        body, mesh=mesh, in_specs=placed, out_specs=P(("groups", "ctx"), None), check_vma=False
    )
```

profile of v0, /device:TPU:0, one launch (start us, length us, event | category | flops | bytes accessed | tf_op | source)
XLA Modules:
  0.0 76.4 jit_solution(9675604063775418156)
XLA Ops:
  6.5 0.0 all-gather.2.cloned.1.call-start
  6.5 1.7 %copy.11 = bf16[128,576]{1,0:T(8,128)(2,1)} copy(bf16[128,576]{0,1:T(8,128)(2,1)} %param.7) | data formatting | bytes 294912 | tf_op args[1]
  8.2 0.0 all-gather.2.cloned.1.call-update
  8.3 0.6 fusion.22
  9.6 1.3 %reshape.42 = bf16[16,32,192]{2,1,0:T(8,128)(2,1)S(1)} reshape(bf16[16,6144]{1,0:T(8,128)(2,1)} %param.6) | data formatting | bytes 393216 | tf_op jit(solution)/shard_map/reshape | solution.py:21
  10.9 2.9 %fusion.18 = bf16[16,32,512]{2,0,1:T(8,128)(2,1)S(1)} fusion(bf16[32,128,512]{2,1,0:T(8,128)(2,1)} %param.8, bf16[16,32,128]{2,1,0:T(8,128)(2,1)S(1)} %slice.16), kind=kOutput, calls=%fused_computation.20 | convolution fusion | flops 67371008 | bytes 4849664 | tf_op jit(solution)/shard_map/thi,hil->thl/dot_general | solution.py:22
  13.7 41.8 %all-gather.2.cloned.1.call-done = bf16[2048,576]{1,0:T(8,128)(2,1)} async-done(((bf16[128,576]{1,0:T(8,128)(2,1)}), bf16[2048,576]{1,0:T(8,128)(2,1)}) %all-gather.2.cloned.1.call-update) | async-done | bytes 2359312 | tf_op jit(solution)/shard_map/all_gather | solution.py:78
  55.6 10.1 %conditional.1 = (f32[16,32]{1,0:T(8,128)S(1)}, f32[16,32,512]{2,1,0:T(8,128)S(1)}) conditional(s32[]{:T(128)} %convert_element_type.21, (s32[2048]{0:T(1024)S(1)}, s32[16]{0:T(128)S(1)}, bf16[2048,576]{1,0:T(8,128)(2,1)}, bf16[16,32,512]{2,0,1:T(8,128)(2,1)S(1)}, bf16[16,32,192]{2,1,0:T(8,128)(2,1)S(1)}) %tuple.13, () %tuple.14), branch_computations={%region_1.4_spmd, %region_4.5_spmd} | conditional | flops 2290386432 | bytes 41396332 | solution.py:56
  55.6 0.0 copy-start
  55.6 0.1 broadcast_compare_fusion
  55.7 4.6 %copy.10 = bf16[2048,576]{0,1:T(8,128)(2,1)} copy(bf16[2048,576]{1,0:T(8,128)(2,1)} %get-tuple-element.19) | data formatting | bytes 4718592 | tf_op jit(solution)/shard_map
  60.2 0.0 copy-done
  60.2 1.4 %fusion.5 = f32[16,32,2048]{2,1,0:T(8,128)S(1)} fusion(bf16[2048,576]{1,0:T(8,128)(2,1)S(1)} %copy-done, bf16[16,32,512]{2,0,1:T(8,128)(2,1)S(1)} %get-tuple-element.33), kind=kOutput, calls=%fused_computation.6 | convolution fusion | flops 1073741824 | bytes 6815744 | tf_op jit(solution)/shard_map/cond/branch_0_fun/thl,jl->thj/dot_general | solution.py:35
  61.6 2.0 %fusion.23 = (f32[16,32]{1,0:T(8,128)S(1)}, f32[16,32,2048]{2,1,0:T(8,128)S(1)}) fusion(f32[16,32,2048]{2,1,0:T(8,128)S(1)} %fusion.5, bf16[2048,576]{0,1:T(8,128)(2,1)} %copy.10, bf16[16,32,192]{2,1,0:T(8,128)(2,1)S(1)} %get-tuple-element.20, pred[16,2048]{1,0:T(8,128)(4,1)S(1)} %broadcast_compare_fusion), kind=kOutput, calls=%fused_computation.29 | convolution fusion | flops 138411520 | bytes 8816640 | tf_op jit(solution)/shard_map/cond/branch_0_fun/thr,jr->thj/dot_general | solution.py:38
  63.6 0.7 fusion.1
  64.3 1.3 %fusion.10 = f32[16,32,512]{2,1,0:T(8,128)S(1)} fusion(bf16[2048,576]{1,0:T(8,128)(2,1)S(1)} %copy-done, f32[16,32,2048]{2,1,0:T(8,128)S(1)} %get-tuple-element.38, f32[16,32]{1,0:T(8,128)S(1)} %broadcast_maximum_fusion, f32[16,32]{1,0:T(8,128)S(1)} %get-tuple-element.35), kind=kOutput, calls=%fused_computation.11 | convolution fusion | flops 1076101120 | bytes 7356416 | tf_op jit(solution)/shard_map/cond/branch_0_fun/thj,jl->thl/dot_general | solution.py:48
  65.7 0.1 divide_convert_fusion
  65.8 3.1 %fusion.19 = bf16[32,2,8,128]{3,2,1,0:T(8,128)(2,1)S(1)} fusion(bf16[32,512,128]{2,1,0:T(8,128)(2,1)} %param.9, bf16[16,32,512]{2,1,0:T(8,128)(2,1)S(1)} %divide_convert_fusion), kind=kOutput, calls=%fused_computation.22 | convolution fusion | flops 67174400 | bytes 4849664 | tf_op jit(solution)/shard_map/thl,hlc->thc/dot_general | solution.py:81
  68.9 0.7 copy.25
  (5 shorter events, 0.1 us)
Async XLA Ops:
  6.5 49.0 %all-gather.2.cloned.1.call-start = ((), (), s32[]{:S(2)}) async-start(), calls=%async_computation | async-start | bytes 2785280 | tf_op jit(solution)/shard_map/all_gather | solution.py:78
  55.6 4.6 %copy-start = (bf16[2048,576]{1,0:T(8,128)(2,1)S(1)}, bf16[2048,576]{1,0:T(8,128)(2,1)}, u32[]{:S(2)}) copy-start(bf16[2048,576]{1,0:T(8,128)(2,1)} %get-tuple-element.19) | copy-start | bytes 7077892 | tf_op jit(solution)/shard_map/cond
Sparse Core Ops, SparseCore 0:
  9.6 45.8 all-gather.1
where the time goes:
time: 76.7 us; the launch traced here: 76.4 us
  waiting for transfers between devices  41.9 us (55%)
  between operations  14.1 us (18%)
  matrix products  10.6 us (14%)
  local copies, waits for them, and re-layouts  8.22 us (11%)
  other arithmetic  1.61 us (2%)
    all_gather x1, waiting for transfers between devices, body(): lax.all_gather(latents, 'ctx', axis=0, tiled=True)  41.8 us
    another operation x1, local copies, waits for them, and re-layouts  4.55 us
    dot_general x1, matrix products, body(): jnp.einsum('thl,hlc->thc', o_lat, w_uv, preferred_element_type=jnp.float32)  3.07 us
    dot_general x1, matrix products, body(): jnp.einsum('thi,hil->thl', shaped[:, :, :NOPE], w_uk, preferred_element_t...  2.86 us
    dot_general x1, matrix products, work(): jnp.einsum('thr,jr->thj', q_rope, block[:, RANK:], preferred_element_type...  1.96 us
    unnamed x1, local copies, waits for them, and re-layouts  1.7 us
  transfers between devices with their start and end apart: 1, of which 1 were waited for; matrix products, arithmetic and copies ran while one was open for 6% of the time, Pallas kernels for 0%

commit v1 on v0

v1 whole, which is shorter than its diff:
```python
import functools
import math

import jax
import jax.numpy as jnp
from jax import lax
from jax.experimental import pallas as pl
from jax.experimental.pallas import tpu as pltpu
from jax.sharding import PartitionSpec as P

CORES = 2
MESH = pl.DeviceIdType.MESH


def grid_of(count):
    chips = count // CORES
    wide = 1 << (int(math.log2(chips)) // 3)
    return chips // wide, wide


def kernel(
    deep, wide, heads, nope, rank,
    queries, latents, w_uk, w_uv, out,
    keys, raw, q_all, uk, uv, top, total, acc,
    up_sem, side_sem, twin_sem, pass_sem, recv_sem, local_sem, uk_sem,
):
    index = lax.axis_index("ctx")
    core = lax.rem(index, CORES)
    x = lax.rem(index // CORES, wide)
    z = index // (CORES * wide)
    rows = out.shape[0]
    krows = latents.shape[0]
    width = raw.shape[1] // heads
    vdim = out.shape[1] // heads
    span = CORES * krows
    factor = math.log2(math.e) / math.sqrt(width)

    def place(zz, xx, cc):
        return (zz * wide + xx) * CORES + cc

    def slot(block):
        return keys.at[pl.ds(pl.multiple_of(block * krows, krows), krows), :]

    def copy(block, target, send_sem, own=False):
        return pltpu.make_async_remote_copy(
            src_ref=latents if own else slot(block),
            dst_ref=slot(block),
            send_sem=send_sem,
            recv_sem=recv_sem.at[block],
            device_id={"ctx": target},
            device_id_type=MESH,
        )

    twin = place(z, x, 1 - core)
    above = place(lax.rem(z + 1, deep), x, core)
    below = place(lax.rem(z + deep - 1, deep), x, core)
    sides = [lax.rem(x + d, wide) for d in range(1, wide)]

    groups = uk_sem.shape[0]
    per = heads // groups
    raw_copy = pltpu.make_async_copy(queries, raw, local_sem.at[0])
    raw_copy.start()
    uk_copies = []
    for g in range(groups):
        part = pl.ds(g * per, per)
        uk_copies.append(pltpu.make_async_copy(w_uk.at[part], uk.at[part], uk_sem.at[g]))
        uk_copies[-1].start()
    own_copy = pltpu.make_async_copy(latents, slot(index), local_sem.at[1])
    own_copy.start()

    barrier = pltpu.get_barrier_semaphore()

    def greet(target):
        pl.semaphore_signal(barrier, inc=1, device_id={"ctx": target}, device_id_type=MESH)

    greet(twin)
    for side in sides:
        greet(place(z, side, core))

    @pl.when(z + 1 < deep)
    def _():
        greet(above)

    @pl.when(z > 0)
    def _():
        greet(below)

    ends = (z + 1 < deep).astype(jnp.int32) + (z > 0).astype(jnp.int32)
    pl.semaphore_wait(barrier, wide + ends)

    def spread(step, block, own, act):
        @pl.when(z + 1 < deep)
        def _():
            act(copy(block, above, up_sem.at[step], own))

        for d, side in enumerate(sides):
            def to_side():
                act(copy(block, place(z, side, core), side_sem.at[step, d], own))

            if own:
                pl.when(side > x)(to_side)
            else:
                to_side()
        act(copy(block, twin, twin_sem.at[step], own))

    def arrived(block):
        copy(block, twin, twin_sem.at[0]).wait_recv()

    spread(0, index, True, lambda c: c.start())

    raw_copy.wait()
    uv_copy = pltpu.make_async_copy(w_uv, uv, local_sem.at[2])
    for h in range(heads):
        if h % per == 0:
            uk_copies[h // per].wait()
        query = raw[:, h * width:(h + 1) * width]
        lat = jnp.dot(query[:, :nope], uk[h], preferred_element_type=jnp.float32)
        q_all[h * rows:(h + 1) * rows, :rank] = lat.astype(jnp.bfloat16)
        q_all[h * rows:(h + 1) * rows, rank:] = query[:, nope:]
    uv_copy.start()

    parts = 4
    high = heads * rows // parts

    def attend(pair, first):
        start = pl.multiple_of(pair * span, span)
        key = keys[pl.ds(start, span), :]
        value = key[:, :rank]
        for part in range(parts):
            own = pl.ds(part * high, high)
            score = lax.dot_general(
                q_all[own, :], key, (((1,), (1,)), ((), ())), preferred_element_type=jnp.float32
            )
            if first:
                row = lax.broadcasted_iota(jnp.int32, score.shape, 0)
                col = lax.broadcasted_iota(jnp.int32, score.shape, 1)
                limit = core * krows + krows - rows + lax.rem(row, rows)
                score = jnp.where(col <= limit, score, -jnp.inf)
            best = jnp.max(score, axis=1, keepdims=True)
            if not first:
                old = top[own, :1]
                best = jnp.maximum(old, best)
            expo = jnp.exp2((score - best) * factor)
            lanes = expo[:, :128]
            for lane in range(128, span, 128):
                lanes = lanes + expo[:, lane:lane + 128]
            gain = jnp.dot(expo.astype(jnp.bfloat16), value, preferred_element_type=jnp.float32)
            if first:
                total[own, :] = lanes
                acc[own, :] = gain
            else:
                shrink = jnp.exp2((old - best) * factor)
                total[own, :] = total[own, :] * shrink + lanes
                acc[own, :] = acc[own, :] * shrink + gain
            top[own, :] = jnp.broadcast_to(best, (high, 128))

    own_copy.wait()
    arrived(twin)
    attend(index // CORES, True)

    def step_of(step, carry):
        @pl.when(step <= z)
        def _():
            block = place(z - step, x, core)
            arrived(block)
            spread(step, block, False, lambda c: c.start())
            arrived(place(z - step, x, 1 - core))
            attend((z - step) * wide + x, False)

        back = step - 1
        for d, side in enumerate(sides):
            @pl.when(jnp.logical_or(back >= 1, side < x))
            def _():
                block = place(z - back, side, core)
                arrived(block)
                copy(block, twin, pass_sem.at[back, d]).start()
                arrived(place(z - back, side, 1 - core))
                attend((z - back) * wide + side, False)
        return carry

    lax.fori_loop(1, z + 2, step_of, 0)

    uv_copy.wait()
    for h in range(heads):
        own = pl.ds(h * rows, rows)
        whole = jnp.sum(total[own, :], axis=1, keepdims=True)
        mixed = (acc[own, :] * (1.0 / whole)).astype(jnp.bfloat16)
        out[:, h * vdim:(h + 1) * vdim] = jnp.dot(
            mixed, uv[h], preferred_element_type=jnp.float32
        ).astype(out.dtype)

    spread(0, index, True, lambda c: c.wait_send())

    def drain(step, carry):
        @pl.when(step <= z)
        def _():
            spread(step, place(z - step, x, core), False, lambda c: c.wait_send())

        back = step - 1
        for d, side in enumerate(sides):
            @pl.when(jnp.logical_or(back >= 1, side < x))
            def _():
                copy(place(z - back, side, core), twin, pass_sem.at[back, d]).wait_send()
        return carry

    lax.fori_loop(1, z + 2, drain, 0)


def body(count, queries, latents, w_uk, w_uv):
    deep, wide = grid_of(count)
    heads, nope, rank = w_uk.shape
    vdim = w_uv.shape[2]
    rows, krows = queries.shape[0], latents.shape[0]
    dma = pltpu.SemaphoreType.DMA
    lanes = max(wide - 1, 1)
    return pl.pallas_call(
        functools.partial(kernel, deep, wide, heads, nope, rank),
        out_shape=jax.ShapeDtypeStruct((rows, heads * vdim), jnp.bfloat16),
        in_specs=[pl.BlockSpec(memory_space=pl.ANY)] * 4,
        out_specs=pl.BlockSpec(memory_space=pltpu.VMEM),
        scratch_shapes=[
            pltpu.VMEM((count * krows, latents.shape[1]), jnp.bfloat16),
            pltpu.VMEM(queries.shape, jnp.bfloat16),
            pltpu.VMEM((heads * rows, latents.shape[1]), jnp.bfloat16),
            pltpu.VMEM(w_uk.shape, jnp.bfloat16),
            pltpu.VMEM(w_uv.shape, jnp.bfloat16),
            pltpu.VMEM((heads * rows, 128), jnp.float32),
            pltpu.VMEM((heads * rows, 128), jnp.float32),
            pltpu.VMEM((heads * rows, rank), jnp.float32),
            dma((deep,)),
            dma((deep, lanes)),
            dma((deep,)),
            dma((deep, lanes)),
            dma((count,)),
            dma((3,)),
            dma((4,)),
        ],
        compiler_params=pltpu.CompilerParams(
            collective_id=0, has_side_effects=True, vmem_limit_bytes=48 * 1024 * 1024
        ),
    )(queries, latents, w_uk, w_uv)


def solution(mesh):
    placed = (P(("groups", "ctx"), None), P(("groups", "ctx"), None), P(), P())
    return jax.shard_map(
        functools.partial(body, mesh.shape["ctx"]),
        mesh=mesh, in_specs=placed, out_specs=P(("groups", "ctx"), None), check_vma=False,
    )
```

time: 76.7 us -> 36 us (0.47)
  the two profiles are of different devices: /device:TPU:0 before, /device:TPU:27 now
where the time goes in v1:
time: 36 us; the launch traced here: 35.8 us
  Pallas kernels  30.9 us (86%)
  local copies, waits for them, and re-layouts  4.83 us (13%)
    pallas_call x1, Pallas kernels, body(): pl.pallas_call(functools.partial(kernel, deep, wide, heads, nope, rank),...  30.9 us
    unnamed x6, local copies, waits for them, and re-layouts  4.83 us

profile of v1, /device:TPU:27, one launch (start us, length us, event | category | flops | bytes accessed | tf_op | source)
XLA Modules:
  0.0 35.8 jit_solution(9302980570088287945)
XLA Ops:
  0.0 1.1 %copy.5.latents = bf16[128,576]{1,0:T(8,128)(2,1)S(1)} copy(bf16[128,576]{0,1:T(8,128)(2,1)} %param.5) | data formatting | bytes 294912 | tf_op args[1]
  1.1 0.0 copy-start
  1.1 2.2 %copy-done = bf16[32,128,512]{2,1,0:T(8,128)(2,1)S(1)} copy-done((bf16[32,128,512]{2,1,0:T(8,128)(2,1)S(1)}, bf16[32,128,512]{2,1,0:T(8,128)(2,1)}, u32[]{:S(2)}) %copy-start) | copy-done | bytes 4194328
  3.3 0.0 copy-start.1
  3.3 0.9 %copy-done.1 = bf16[16,6144]{1,0:T(8,128)(2,1)S(1)} copy-done((bf16[16,6144]{1,0:T(8,128)(2,1)S(1)}, bf16[16,6144]{1,0:T(8,128)(2,1)}, u32[]{:S(2)}) %copy-start.1) | copy-done | bytes 196632
  4.2 30.9 %shard_map.46 = bf16[16,4096]{1,0:T(8,128)(2,1)S(1)} custom-call(bf16[16,6144]{1,0:T(8,128)(2,1)S(1)} %copy-done.1, bf16[128,576]{1,0:T(8,128)(2,1)S(1)} %copy.5.latents, bf16[32,128,512]{2,1,0:T(8,128)(2,1)S(1)} %copy-done, bf16[32,512,128]{2,1,0:T(8,128)(2,1)} %w_uv.1), custom_call_target="tpu_custom_call" | custom-call | tf_op jit(solution)/shard_map/pallas_call | solution.py:216
  35.1 0.7 %copy.7 = bf16[16,4096]{1,0:T(8,128)(2,1)} copy(bf16[16,4096]{1,0:T(8,128)(2,1)S(1)} %shard_map.46) | data formatting | bytes 262144
Async XLA Ops:
  1.1 2.2 %copy-start = (bf16[32,128,512]{2,1,0:T(8,128)(2,1)S(1)}, bf16[32,128,512]{2,1,0:T(8,128)(2,1)}, u32[]{:S(2)}) copy-start(bf16[32,128,512]{2,1,0:T(8,128)(2,1)} %w_uk.1) | copy-start | bytes 12582916
  3.3 0.9 %copy-start.1 = (bf16[16,6144]{1,0:T(8,128)(2,1)S(1)}, bf16[16,6144]{1,0:T(8,128)(2,1)}, u32[]{:S(2)}) copy-start(bf16[16,6144]{1,0:T(8,128)(2,1)} %queries.1) | copy-start | bytes 589828

commit v2 on v1

--- a/solution.py
+++ b/solution.py
@@ -29,7 +29,7 @@
     x = lax.rem(index // CORES, wide)
     z = index // (CORES * wide)
     rows = out.shape[0]
-    krows = latents.shape[0]
+    krows = latents.shape[1]
     width = raw.shape[1] // heads
     vdim = out.shape[1] // heads
     span = CORES * krows
@@ -39,7 +39,7 @@
         return (zz * wide + xx) * CORES + cc
 
     def slot(block):
-        return keys.at[pl.ds(pl.multiple_of(block * krows, krows), krows), :]
+        return keys.at[block]
 
     def copy(block, target, send_sem, own=False):
         return pltpu.make_async_remote_copy(
@@ -119,18 +119,18 @@
         q_all[h * rows:(h + 1) * rows, rank:] = query[:, nope:]
     uv_copy.start()
 
-    parts = 4
+    parts = 2
     high = heads * rows // parts
 
     def attend(pair, first):
-        start = pl.multiple_of(pair * span, span)
-        key = keys[pl.ds(start, span), :]
-        value = key[:, :rank]
-        for part in range(parts):
-            own = pl.ds(part * high, high)
-            score = lax.dot_general(
-                q_all[own, :], key, (((1,), (1,)), ((), ())), preferred_element_type=jnp.float32
-            )
+        blocks = [keys[pair * CORES + c] for c in range(CORES)]
+        key = jnp.concatenate(blocks, axis=1)
+        value = key[:rank, :].T
+        owns = [pl.ds(part * high, high) for part in range(parts)]
+        scores = [
+            jnp.dot(q_all[own, :], key, preferred_element_type=jnp.float32) for own in owns
+        ]
+        for own, score in zip(owns, scores):
             if first:
                 row = lax.broadcasted_iota(jnp.int32, score.shape, 0)
                 col = lax.broadcasted_iota(jnp.int32, score.shape, 1)
@@ -210,7 +210,8 @@
     deep, wide = grid_of(count)
     heads, nope, rank = w_uk.shape
     vdim = w_uv.shape[2]
-    rows, krows = queries.shape[0], latents.shape[0]
+    rows = queries.shape[0]
+    krows, width = latents.shape
     dma = pltpu.SemaphoreType.DMA
     lanes = max(wide - 1, 1)
     return pl.pallas_call(
@@ -219,9 +220,9 @@
         in_specs=[pl.BlockSpec(memory_space=pl.ANY)] * 4,
         out_specs=pl.BlockSpec(memory_space=pltpu.VMEM),
         scratch_shapes=[
-            pltpu.VMEM((count * krows, latents.shape[1]), jnp.bfloat16),
+            pltpu.VMEM((count, width, krows), jnp.bfloat16),
             pltpu.VMEM(queries.shape, jnp.bfloat16),
-            pltpu.VMEM((heads * rows, latents.shape[1]), jnp.bfloat16),
+            pltpu.VMEM((heads * rows, width), jnp.bfloat16),
             pltpu.VMEM(w_uk.shape, jnp.bfloat16),
             pltpu.VMEM(w_uv.shape, jnp.bfloat16),
             pltpu.VMEM((heads * rows, 128), jnp.float32),
@@ -236,9 +237,9 @@
             dma((4,)),
         ],
         compiler_params=pltpu.CompilerParams(
-            collective_id=0, has_side_effects=True, vmem_limit_bytes=48 * 1024 * 1024
+            collective_id=0, has_side_effects=True, vmem_limit_bytes=60 * 1024 * 1024
         ),
-    )(queries, latents, w_uk, w_uv)
+    )(queries, latents.T, w_uk, w_uv)
 
 
 def solution(mesh):

time: 36 us -> 24.1 us (0.67)
  the two profiles are of different devices: /device:TPU:27 before, /device:TPU:25 now
where the time goes in v2:
time: 24.1 us; the launch traced here: 24 us
  Pallas kernels  22.4 us (93%)
  local copies, waits for them, and re-layouts  1.57 us (7%)
    pallas_call x1, Pallas kernels, body(): pl.pallas_call(functools.partial(kernel, deep, wide, heads, nope, rank),...  22.4 us
    unnamed x1, local copies, waits for them, and re-layouts  1.57 us

profile of v2, /device:TPU:25, one launch (start us, length us, event | category | flops | bytes accessed | tf_op | source)
XLA Modules:
  0.0 24.0 jit_solution(13113123056667144622)
XLA Ops:
  0.0 22.4 %shard_map.46 = bf16[16,4096]{1,0:T(8,128)(2,1)} custom-call(bf16[16,6144]{1,0:T(8,128)(2,1)} %queries.1, bf16[576,128]{1,0:T(8,128)(2,1)} %bitcast.1, bf16[32,128,512]{2,1,0:T(8,128)(2,1)} %w_uk.1, bf16[32,512,128]{2,1,0:T(8,128)(2,1)} %w_uv.1), custom_call_target="tpu_custom_call" | custom-call | tf_op jit(solution)/shard_map/pallas_call | solution.py:217
  22.4 1.6 %copy.6 = bf16[16,4096]{1,0:T(8,128)(2,1)} copy(bf16[16,4096]{1,0:T(8,128)(2,1)} %shard_map.46) | data formatting | bytes 262144

commit v3 on v2

--- a/solution.py
+++ b/solution.py
@@ -9,6 +9,7 @@
 from jax.sharding import PartitionSpec as P
 
 CORES = 2
+PIECES = 2
 MESH = pl.DeviceIdType.MESH
 
 
@@ -38,15 +39,17 @@
     def place(zz, xx, cc):
         return (zz * wide + xx) * CORES + cc
 
-    def slot(block):
-        return keys.at[block]
-
-    def copy(block, target, send_sem, own=False):
+    def piece_of(piece):
+        size = keys.shape[1] // PIECES
+        return pl.ds(piece * size, size)
+
+    def copy(block, piece, target, send_sem, own=False):
+        there = keys.at[block, piece_of(piece), :]
         return pltpu.make_async_remote_copy(
-            src_ref=latents if own else slot(block),
-            dst_ref=slot(block),
+            src_ref=latents.at[piece_of(piece), :] if own else there,
+            dst_ref=there,
             send_sem=send_sem,
-            recv_sem=recv_sem.at[block],
+            recv_sem=recv_sem.at[block, piece],
             device_id={"ctx": target},
             device_id_type=MESH,
         )
@@ -65,7 +68,7 @@
         part = pl.ds(g * per, per)
         uk_copies.append(pltpu.make_async_copy(w_uk.at[part], uk.at[part], uk_sem.at[g]))
         uk_copies[-1].start()
-    own_copy = pltpu.make_async_copy(latents, slot(index), local_sem.at[1])
+    own_copy = pltpu.make_async_copy(latents, keys.at[index], local_sem.at[1])
     own_copy.start()
 
     barrier = pltpu.get_barrier_semaphore()
@@ -88,25 +91,47 @@
     ends = (z + 1 < deep).astype(jnp.int32) + (z > 0).astype(jnp.int32)
     pl.semaphore_wait(barrier, wide + ends)
 
-    def spread(step, block, own, act):
+    def spread(step, piece, own, act):
+        block = place(z - step, x, core)
+
         @pl.when(z + 1 < deep)
         def _():
-            act(copy(block, above, up_sem.at[step], own))
+            act(copy(block, piece, above, up_sem.at[step, piece], own))
 
         for d, side in enumerate(sides):
             def to_side():
-                act(copy(block, place(z, side, core), side_sem.at[step, d], own))
+                act(copy(block, piece, place(z, side, core), side_sem.at[step, d, piece], own))
 
             if own:
                 pl.when(side > x)(to_side)
             else:
                 to_side()
-        act(copy(block, twin, twin_sem.at[step], own))
-
-    def arrived(block):
-        copy(block, twin, twin_sem.at[0]).wait_recv()
-
-    spread(0, index, True, lambda c: c.start())
+        act(copy(block, piece, twin, twin_sem.at[step, piece], own))
+
+    def arrived(block, piece):
+        copy(block, piece, twin, twin_sem.at[0, 0]).wait_recv()
+
+    def whole(block):
+        for piece in range(PIECES):
+            arrived(block, piece)
+
+    def needed(step, side):
+        return jnp.logical_or(step >= 1, side < x)
+
+    def column(step, piece):
+        arrived(place(z - step, x, core), piece)
+        spread(step, piece, False, lambda c: c.start())
+
+    def across(step, piece):
+        for d, side in enumerate(sides):
+            @pl.when(needed(step, side))
+            def _():
+                block = place(z - step, side, core)
+                arrived(block, piece)
+                copy(block, piece, twin, pass_sem.at[step, d, piece]).start()
+
+    for piece in range(PIECES):
+        spread(0, piece, True, lambda c: c.start())
 
     raw_copy.wait()
     uv_copy = pltpu.make_async_copy(w_uv, uv, local_sem.at[2])
@@ -154,56 +179,76 @@
                 acc[own, :] = acc[own, :] * shrink + gain
             top[own, :] = jnp.broadcast_to(best, (high, 128))
 
+    def attend_column(step):
+        whole(place(z - step, x, 1 - core))
+        attend((z - step) * wide + x, False)
+
+    def attend_across(step):
+        for side in sides:
+            @pl.when(needed(step, side))
+            def _():
+                whole(place(z - step, side, 1 - core))
+                attend((z - step) * wide + side, False)
+
     own_copy.wait()
-    arrived(twin)
+    whole(twin)
     attend(index // CORES, True)
 
     def step_of(step, carry):
-        @pl.when(step <= z)
+        column(step, 0)
+        across(step - 1, 0)
+
+        @pl.when(step >= 2)
         def _():
-            block = place(z - step, x, core)
-            arrived(block)
-            spread(step, block, False, lambda c: c.start())
-            arrived(place(z - step, x, 1 - core))
-            attend((z - step) * wide + x, False)
-
-        back = step - 1
-        for d, side in enumerate(sides):
-            @pl.when(jnp.logical_or(back >= 1, side < x))
-            def _():
-                block = place(z - back, side, core)
-                arrived(block)
-                copy(block, twin, pass_sem.at[back, d]).start()
-                arrived(place(z - back, side, 1 - core))
-                attend((z - back) * wide + side, False)
+            attend_column(step - 1)
+
+        for piece in range(1, PIECES):
+            column(step, piece)
+            across(step - 1, piece)
+
+        @pl.when(step >= 2)
+        def _():
+            attend_across(step - 2)
+
         return carry
 
-    lax.fori_loop(1, z + 2, step_of, 0)
+    lax.fori_loop(1, z + 1, step_of, 0)
+    across(z, 0)
+
+    @pl.when(z >= 1)
+    def _():
+        attend_column(z)
+        attend_across(z - 1)
+
+    for piece in range(1, PIECES):
+        across(z, piece)
+    attend_across(z)
 
     uv_copy.wait()
     for h in range(heads):
         own = pl.ds(h * rows, rows)
-        whole = jnp.sum(total[own, :], axis=1, keepdims=True)
-        mixed = (acc[own, :] * (1.0 / whole)).astype(jnp.bfloat16)
+        mass = jnp.sum(total[own, :], axis=1, keepdims=True)
+        mixed = (acc[own, :] * (1.0 / mass)).astype(jnp.bfloat16)
         out[:, h * vdim:(h + 1) * vdim] = jnp.dot(
             mixed, uv[h], preferred_element_type=jnp.float32
         ).astype(out.dtype)
 
-    spread(0, index, True, lambda c: c.wait_send())
-
     def drain(step, carry):
-        @pl.when(step <= z)
-        def _():
-            spread(step, place(z - step, x, core), False, lambda c: c.wait_send())
-
-        back = step - 1
-        for d, side in enumerate(sides):
-            @pl.when(jnp.logical_or(back >= 1, side < x))
+        for piece in range(PIECES):
+            @pl.when(step >= 1)
             def _():
-                copy(place(z - back, side, core), twin, pass_sem.at[back, d]).wait_send()
+                spread(step, piece, False, lambda c: c.wait_send())
+
+            for d, side in enumerate(sides):
+                @pl.when(needed(step, side))
+                def _():
+                    block = place(z - step, side, core)
+                    copy(block, piece, twin, pass_sem.at[step, d, piece]).wait_send()
         return carry
 
-    lax.fori_loop(1, z + 2, drain, 0)
+    for piece in range(PIECES):
+        spread(0, piece, True, lambda c: c.wait_send())
+    lax.fori_loop(0, z + 1, drain, 0)
 
 
 def body(count, queries, latents, w_uk, w_uv):
@@ -217,7 +262,7 @@
     return pl.pallas_call(
         functools.partial(kernel, deep, wide, heads, nope, rank),
         out_shape=jax.ShapeDtypeStruct((rows, heads * vdim), jnp.bfloat16),
-        in_specs=[pl.BlockSpec(memory_space=pl.ANY)] * 4,
+        in_specs=[pl.BlockSpec(memory_space=pltpu.HBM)] * 4,
         out_specs=pl.BlockSpec(memory_space=pltpu.VMEM),
         scratch_shapes=[
             pltpu.VMEM((count, width, krows), jnp.bfloat16),
@@ -228,11 +273,11 @@
             pltpu.VMEM((heads * rows, 128), jnp.float32),
             pltpu.VMEM((heads * rows, 128), jnp.float32),
             pltpu.VMEM((heads * rows, rank), jnp.float32),
-            dma((deep,)),
-            dma((deep, lanes)),
-            dma((deep,)),
-            dma((deep, lanes)),
-            dma((count,)),
+            dma((deep, PIECES)),
+            dma((deep, lanes, PIECES)),
+            dma((deep, PIECES)),
+            dma((deep, lanes, PIECES)),
+            dma((count, PIECES)),
             dma((3,)),
             dma((4,)),
         ],

time: 24.1 us -> 23.5 us (0.975)
  Pallas kernels: 22.4 us -> 21.7 us
    pallas_call x1, Pallas kernels: 22.4 us -> 21.7 us  [body(): pl.pallas_call(functools.partial(kernel, deep, wide, heads, nope, rank),...]
where the time goes in v3:
time: 23.5 us; the launch traced here: 23.3 us
  Pallas kernels  21.7 us (92%)
  local copies, waits for them, and re-layouts  1.57 us (7%)
    pallas_call x1, Pallas kernels, body(): pl.pallas_call(functools.partial(kernel, deep, wide, heads, nope, rank),...  21.7 us
    unnamed x1, local copies, waits for them, and re-layouts  1.57 us

profile of v3, /device:TPU:25, one launch (start us, length us, event | category | flops | bytes accessed | tf_op | source)
XLA Modules:
  0.0 23.3 jit_solution(16539475666157250321)
XLA Ops:
  0.0 21.7 %shard_map.46 = bf16[16,4096]{1,0:T(8,128)(2,1)} custom-call(bf16[16,6144]{1,0:T(8,128)(2,1)} %queries.1, bf16[576,128]{1,0:T(8,128)(2,1)} %bitcast.1, bf16[32,128,512]{2,1,0:T(8,128)(2,1)} %w_uk.1, bf16[32,512,128]{2,1,0:T(8,128)(2,1)} %w_uv.1), custom_call_target="tpu_custom_call" | custom-call | tf_op jit(solution)/shard_map/pallas_call | solution.py:262
  21.8 1.6 %copy.6 = bf16[16,4096]{1,0:T(8,128)(2,1)} copy(bf16[16,4096]{1,0:T(8,128)(2,1)} %shard_map.46) | data formatting | bytes 262144

commit v4 on v3

--- a/solution.py
+++ b/solution.py
@@ -9,7 +9,7 @@
 from jax.sharding import PartitionSpec as P
 
 CORES = 2
-PIECES = 2
+PIECES = 4
 MESH = pl.DeviceIdType.MESH
 
 
@@ -195,14 +195,15 @@
     attend(index // CORES, True)
 
     def step_of(step, carry):
-        column(step, 0)
-        across(step - 1, 0)
+        for piece in range(PIECES // 2):
+            column(step, piece)
+            across(step - 1, piece)
 
         @pl.when(step >= 2)
         def _():
             attend_column(step - 1)
 
-        for piece in range(1, PIECES):
+        for piece in range(PIECES // 2, PIECES):
             column(step, piece)
             across(step - 1, piece)
 
@@ -213,14 +214,15 @@
         return carry
 
     lax.fori_loop(1, z + 1, step_of, 0)
-    across(z, 0)
+    for piece in range(PIECES // 2):
+        across(z, piece)
 
     @pl.when(z >= 1)
     def _():
         attend_column(z)
         attend_across(z - 1)
 
-    for piece in range(1, PIECES):
+    for piece in range(PIECES // 2, PIECES):
         across(z, piece)
     attend_across(z)
 
@@ -282,7 +284,7 @@
             dma((4,)),
         ],
         compiler_params=pltpu.CompilerParams(
-            collective_id=0, has_side_effects=True, vmem_limit_bytes=60 * 1024 * 1024
+            collective_id=0, has_side_effects=True, vmem_limit_bytes=55050 * 1024
         ),
     )(queries, latents.T, w_uk, w_uv)
 

time: 23.5 us -> 21.9 us (0.932)
  local copies, waits for them, and re-layouts: 1.57 us -> 0.66 us
  Pallas kernels: 21.7 us -> 21 us
    unnamed x1, local copies, waits for them, and re-layouts: 1.57 us -> 0.66 us
    pallas_call x1, Pallas kernels: 21.7 us -> 21 us  [body(): pl.pallas_call(functools.partial(kernel, deep, wide, heads, nope, rank),...]
where the time goes in v4:
time: 21.9 us; the launch traced here: 21.7 us
  Pallas kernels  21 us (96%)
  local copies, waits for them, and re-layouts  0.66 us (3%)
    pallas_call x1, Pallas kernels, body(): pl.pallas_call(functools.partial(kernel, deep, wide, heads, nope, rank),...  21 us
    unnamed x1, local copies, waits for them, and re-layouts  0.66 us

profile of v4, /device:TPU:25, one launch (start us, length us, event | category | flops | bytes accessed | tf_op | source)
XLA Modules:
  0.0 21.7 jit_solution(9414484782253092482)
XLA Ops:
  0.0 21.0 %shard_map.46 = bf16[16,4096]{1,0:T(8,128)(2,1)S(1)} custom-call(bf16[16,6144]{1,0:T(8,128)(2,1)} %queries.1, bf16[576,128]{1,0:T(8,128)(2,1)} %bitcast.1, bf16[32,128,512]{2,1,0:T(8,128)(2,1)} %w_uk.1, bf16[32,512,128]{2,1,0:T(8,128)(2,1)} %w_uv.1), custom_call_target="tpu_custom_call" | custom-call | tf_op jit(solution)/shard_map/pallas_call | solution.py:264
  21.1 0.7 %copy.6 = bf16[16,4096]{1,0:T(8,128)(2,1)} copy(bf16[16,4096]{1,0:T(8,128)(2,1)S(1)} %shard_map.46) | data formatting | bytes 262144

commit v5 on v4

--- a/solution.py
+++ b/solution.py
@@ -10,6 +10,7 @@
 
 CORES = 2
 PIECES = 4
+HALF = PIECES // 2
 MESH = pl.DeviceIdType.MESH
 
 
@@ -23,7 +24,7 @@
     deep, wide, heads, nope, rank,
     queries, latents, w_uk, w_uv, out,
     keys, raw, q_all, uk, uv, top, total, acc,
-    up_sem, side_sem, twin_sem, pass_sem, recv_sem, local_sem, uk_sem,
+    up_sem, side_sem, twin_sem, pass_sem, far_sem, recv_sem, local_sem, uk_sem,
 ):
     index = lax.axis_index("ctx")
     core = lax.rem(index, CORES)
@@ -102,8 +103,12 @@
             def to_side():
                 act(copy(block, piece, place(z, side, core), side_sem.at[step, d, piece], own))
 
-            if own:
+            if own and piece >= HALF:
+                pl.when(jnp.logical_or(side > x, z == 0))(to_side)
+            elif own:
                 pl.when(side > x)(to_side)
+            elif piece >= HALF:
+                pl.when(step < z)(to_side)
             else:
                 to_side()
         act(copy(block, piece, twin, twin_sem.at[step, piece], own))
@@ -121,14 +126,30 @@
     def column(step, piece):
         arrived(place(z - step, x, core), piece)
         spread(step, piece, False, lambda c: c.start())
+
+    def hand(step, piece, d, side, act):
+        act(copy(place(z - step, side, core), piece, twin, pass_sem.at[step, d, piece]))
+
+    def relay(piece, d, side, act):
+        @pl.when(z + 1 < deep)
+        def _():
+            act(copy(place(0, side, core), piece, above, far_sem.at[d, piece]))
 
     def across(step, piece):
         for d, side in enumerate(sides):
             @pl.when(needed(step, side))
             def _():
-                block = place(z - step, side, core)
-                arrived(block, piece)
-                copy(block, piece, twin, pass_sem.at[step, d, piece]).start()
+                arrived(place(z - step, side, core), piece)
+                hand(step, piece, d, side, lambda c: c.start())
+
+    def far(piece):
+        for d, side in enumerate(sides):
+            arrived(place(0, side, core), piece)
+            relay(piece, d, side, lambda c: c.start())
+
+            @pl.when(needed(z, side))
+            def _():
+                hand(z, piece, d, side, lambda c: c.start())
 
     for piece in range(PIECES):
         spread(0, piece, True, lambda c: c.start())
@@ -194,17 +215,21 @@
     whole(twin)
     attend(index // CORES, True)
 
+    low, up = range(HALF), range(HALF, PIECES)
+
     def step_of(step, carry):
-        for piece in range(PIECES // 2):
+        for piece in low:
             column(step, piece)
-            across(step - 1, piece)
 
         @pl.when(step >= 2)
         def _():
+            for piece in up:
+                across(step - 2, piece)
             attend_column(step - 1)
 
-        for piece in range(PIECES // 2, PIECES):
+        for piece in up:
             column(step, piece)
+        for piece in low:
             across(step - 1, piece)
 
         @pl.when(step >= 2)
@@ -214,16 +239,22 @@
         return carry
 
     lax.fori_loop(1, z + 1, step_of, 0)
-    for piece in range(PIECES // 2):
-        across(z, piece)
 
     @pl.when(z >= 1)
     def _():
+        for piece in up:
+            across(z - 1, piece)
         attend_column(z)
+
+    for piece in low:
+        across(z, piece)
+    for piece in up:
+        far(piece)
+
+    @pl.when(z >= 1)
+    def _():
         attend_across(z - 1)
 
-    for piece in range(PIECES // 2, PIECES):
-        across(z, piece)
     attend_across(z)
 
     uv_copy.wait()
@@ -244,13 +275,15 @@
             for d, side in enumerate(sides):
                 @pl.when(needed(step, side))
                 def _():
-                    block = place(z - step, side, core)
-                    copy(block, piece, twin, pass_sem.at[step, d, piece]).wait_send()
+                    hand(step, piece, d, side, lambda c: c.wait_send())
         return carry
 
     for piece in range(PIECES):
         spread(0, piece, True, lambda c: c.wait_send())
     lax.fori_loop(0, z + 1, drain, 0)
+    for piece in up:
+        for d, side in enumerate(sides):
+            relay(piece, d, side, lambda c: c.wait_send())
 
 
 def body(count, queries, latents, w_uk, w_uv):
@@ -279,6 +312,7 @@
             dma((deep, lanes, PIECES)),
             dma((deep, PIECES)),
             dma((deep, lanes, PIECES)),
+            dma((lanes, PIECES)),
             dma((count, PIECES)),
             dma((3,)),
             dma((4,)),

time: 21.9 us -> 19.9 us (0.909)
  Pallas kernels: 21 us -> 19.1 us
    pallas_call x1, Pallas kernels: 21 us -> 19.1 us  [body(): pl.pallas_call(functools.partial(kernel, deep, wide, heads, nope, rank),...]
where the time goes in v5:
time: 19.9 us; the launch traced here: 19.8 us
  Pallas kernels  19.1 us (96%)
  local copies, waits for them, and re-layouts  0.66 us (3%)
    pallas_call x1, Pallas kernels, body(): pl.pallas_call(functools.partial(kernel, deep, wide, heads, nope, rank),...  19.1 us
    unnamed x1, local copies, waits for them, and re-layouts  0.66 us

profile of v5, /device:TPU:25, one launch (start us, length us, event | category | flops | bytes accessed | tf_op | source)
XLA Modules:
  0.0 19.8 jit_solution(15869058986076217831)
XLA Ops:
  0.0 19.1 %shard_map.46 = bf16[16,4096]{1,0:T(8,128)(2,1)S(1)} custom-call(bf16[16,6144]{1,0:T(8,128)(2,1)} %queries.1, bf16[576,128]{1,0:T(8,128)(2,1)} %bitcast.1, bf16[32,128,512]{2,1,0:T(8,128)(2,1)} %w_uk.1, bf16[32,512,128]{2,1,0:T(8,128)(2,1)} %w_uv.1), custom_call_target="tpu_custom_call" | custom-call | tf_op jit(solution)/shard_map/pallas_call | solution.py:297
  19.1 0.7 %copy.6 = bf16[16,4096]{1,0:T(8,128)(2,1)} copy(bf16[16,4096]{1,0:T(8,128)(2,1)S(1)} %shard_map.46) | data formatting | bytes 262144

commit v6 on v5

--- a/solution.py
+++ b/solution.py
@@ -11,6 +11,7 @@
 CORES = 2
 PIECES = 4
 HALF = PIECES // 2
+LAST = PIECES - 1
 MESH = pl.DeviceIdType.MESH
 
 
@@ -60,6 +61,23 @@
     below = place(lax.rem(z + deep - 1, deep), x, core)
     sides = [lax.rem(x + d, wide) for d in range(1, wide)]
 
+    barrier = pltpu.get_barrier_semaphore()
+
+    def greet(target):
+        pl.semaphore_signal(barrier, inc=1, device_id={"ctx": target}, device_id_type=MESH)
+
+    greet(twin)
+    for side in sides:
+        greet(place(z, side, core))
+
+    @pl.when(z + 1 < deep)
+    def _():
+        greet(above)
+
+    @pl.when(z > 0)
+    def _():
+        greet(below)
+
     groups = uk_sem.shape[0]
     per = heads // groups
     raw_copy = pltpu.make_async_copy(queries, raw, local_sem.at[0])
@@ -72,23 +90,6 @@
     own_copy = pltpu.make_async_copy(latents, keys.at[index], local_sem.at[1])
     own_copy.start()
 
-    barrier = pltpu.get_barrier_semaphore()
-
-    def greet(target):
-        pl.semaphore_signal(barrier, inc=1, device_id={"ctx": target}, device_id_type=MESH)
-
-    greet(twin)
-    for side in sides:
-        greet(place(z, side, core))
-
-    @pl.when(z + 1 < deep)
-    def _():
-        greet(above)
-
-    @pl.when(z > 0)
-    def _():
-        greet(below)
-
     ends = (z + 1 < deep).astype(jnp.int32) + (z > 0).astype(jnp.int32)
     pl.semaphore_wait(barrier, wide + ends)
 
@@ -103,12 +104,14 @@
             def to_side():
                 act(copy(block, piece, place(z, side, core), side_sem.at[step, d, piece], own))
 
-            if own and piece >= HALF:
+            if own and piece >= LAST:
                 pl.when(jnp.logical_or(side > x, z == 0))(to_side)
             elif own:
                 pl.when(side > x)(to_side)
+            elif piece >= LAST:
+                pl.when(step < z)(to_side)
             elif piece >= HALF:
-                pl.when(step < z)(to_side)
+                pl.when(jnp.logical_or(step < z, side < x))(to_side)
             else:
                 to_side()
         act(copy(block, piece, twin, twin_sem.at[step, piece], own))
@@ -130,8 +133,11 @@
     def hand(step, piece, d, side, act):
         act(copy(place(z - step, side, core), piece, twin, pass_sem.at[step, d, piece]))
 
+    def by_column(piece, side):
+        return jnp.logical_or(side < x, piece >= LAST)
+
     def relay(piece, d, side, act):
-        @pl.when(z + 1 < deep)
+        @pl.when(jnp.logical_and(by_column(piece, side), z + 1 < deep))
         def _():
             act(copy(place(0, side, core), piece, above, far_sem.at[d, piece]))
 
@@ -144,7 +150,10 @@
 
     def far(piece):
         for d, side in enumerate(sides):
-            arrived(place(0, side, core), piece)
+            @pl.when(jnp.logical_or(by_column(piece, side), needed(z, side)))
+            def _():
+                arrived(place(0, side, core), piece)
+
             relay(piece, d, side, lambda c: c.start())
 
             @pl.when(needed(z, side))
@@ -246,14 +255,13 @@
             across(z - 1, piece)
         attend_column(z)
 
-    for piece in low:
+    for piece in range(HALF):
         across(z, piece)
-    for piece in up:
-        far(piece)
-
-    @pl.when(z >= 1)
-    def _():
-        attend_across(z - 1)
+        far(HALF + piece)
+        if piece == 0:
+            @pl.when(z >= 1)
+            def _():
+                attend_across(z - 1)
 
     attend_across(z)
 

time: 19.9 us -> 21.5 us (1.080)
  Pallas kernels: 19.1 us -> 20.7 us
    pallas_call x1, Pallas kernels: 19.1 us -> 20.7 us  [body(): pl.pallas_call(functools.partial(kernel, deep, wide, heads, nope, rank),...]
where the time goes in v6:
time: 21.5 us; the launch traced here: 21.4 us
  Pallas kernels  20.7 us (96%)
  local copies, waits for them, and re-layouts  0.66 us (3%)
    pallas_call x1, Pallas kernels, body(): pl.pallas_call(functools.partial(kernel, deep, wide, heads, nope, rank),...  20.7 us
    unnamed x1, local copies, waits for them, and re-layouts  0.66 us

profile of v6, /device:TPU:25, one launch (start us, length us, event | category | flops | bytes accessed | tf_op | source)
XLA Modules:
  0.0 21.4 jit_solution(15764065242749873149)
XLA Ops:
  0.0 20.7 %shard_map.46 = bf16[16,4096]{1,0:T(8,128)(2,1)S(1)} custom-call(bf16[16,6144]{1,0:T(8,128)(2,1)} %queries.1, bf16[576,128]{1,0:T(8,128)(2,1)} %bitcast.1, bf16[32,128,512]{2,1,0:T(8,128)(2,1)} %w_uk.1, bf16[32,512,128]{2,1,0:T(8,128)(2,1)} %w_uv.1), custom_call_target="tpu_custom_call" | custom-call | tf_op jit(solution)/shard_map/pallas_call | solution.py:305
  20.7 0.7 %copy.6 = bf16[16,4096]{1,0:T(8,128)(2,1)} copy(bf16[16,4096]{1,0:T(8,128)(2,1)S(1)} %shard_map.46) | data formatting | bytes 262144

commit v7 on v5

--- a/solution.py
+++ b/solution.py
@@ -166,6 +166,7 @@
     uv_copy.start()
 
     parts = 2
+    lanes = top.shape[1]
     high = heads * rows // parts
 
     def attend(pair, first):
@@ -182,23 +183,27 @@
                 col = lax.broadcasted_iota(jnp.int32, score.shape, 1)
                 limit = core * krows + krows - rows + lax.rem(row, rows)
                 score = jnp.where(col <= limit, score, -jnp.inf)
-            best = jnp.max(score, axis=1, keepdims=True)
+            best = jnp.broadcast_to(jnp.max(score, axis=1, keepdims=True), (high, lanes))
             if not first:
-                old = top[own, :1]
+                old = top[own, :]
                 best = jnp.maximum(old, best)
-            expo = jnp.exp2((score - best) * factor)
-            lanes = expo[:, :128]
-            for lane in range(128, span, 128):
-                lanes = lanes + expo[:, lane:lane + 128]
-            gain = jnp.dot(expo.astype(jnp.bfloat16), value, preferred_element_type=jnp.float32)
+            expos = [
+                jnp.exp2((score[:, lane:lane + lanes] - best) * factor)
+                for lane in range(0, span, lanes)
+            ]
+            mass = functools.reduce(jnp.add, expos)
+            weight = jnp.concatenate([e.astype(jnp.bfloat16) for e in expos], axis=1)
+            gain = jnp.dot(weight, value, preferred_element_type=jnp.float32)
             if first:
-                total[own, :] = lanes
+                total[own, :] = mass
                 acc[own, :] = gain
             else:
                 shrink = jnp.exp2((old - best) * factor)
-                total[own, :] = total[own, :] * shrink + lanes
-                acc[own, :] = acc[own, :] * shrink + gain
-            top[own, :] = jnp.broadcast_to(best, (high, 128))
+                total[own, :] = total[own, :] * shrink + mass
+                for lane in range(0, rank, lanes):
+                    part = slice(lane, lane + lanes)
+                    acc[own, part] = acc[own, part] * shrink + gain[:, part]
+            top[own, :] = best
 
     def attend_column(step):
         whole(place(z - step, x, 1 - core))

time: 19.9 us -> 19.8 us (level)
  no operation moved by 1% of the time
where the time goes in v7:
time: 19.8 us; the launch traced here: 19.7 us
  Pallas kernels  19 us (96%)
  local copies, waits for them, and re-layouts  0.66 us (3%)
    pallas_call x1, Pallas kernels, body(): pl.pallas_call(functools.partial(kernel, deep, wide, heads, nope, rank),...  19 us
    unnamed x1, local copies, waits for them, and re-layouts  0.66 us

profile of v7, /device:TPU:25, one launch (start us, length us, event | category | flops | bytes accessed | tf_op | source)
XLA Modules:
  0.0 19.7 jit_solution(2645272275813151450)
XLA Ops:
  0.0 19.0 %shard_map.46 = bf16[16,4096]{1,0:T(8,128)(2,1)S(1)} custom-call(bf16[16,6144]{1,0:T(8,128)(2,1)} %queries.1, bf16[576,128]{1,0:T(8,128)(2,1)} %bitcast.1, bf16[32,128,512]{2,1,0:T(8,128)(2,1)} %w_uk.1, bf16[32,512,128]{2,1,0:T(8,128)(2,1)} %w_uv.1), custom_call_target="tpu_custom_call" | custom-call | tf_op jit(solution)/shard_map/pallas_call | solution.py:302
  19.0 0.7 %copy.6 = bf16[16,4096]{1,0:T(8,128)(2,1)} copy(bf16[16,4096]{1,0:T(8,128)(2,1)S(1)} %shard_map.46) | data formatting | bytes 262144

commit v8 on v7

--- a/solution.py
+++ b/solution.py
@@ -263,13 +263,17 @@
     attend_across(z)
 
     uv_copy.wait()
-    for h in range(heads):
-        own = pl.ds(h * rows, rows)
+    group = math.gcd(heads, 2)
+    for first in range(0, heads, group):
+        own = pl.ds(first * rows, group * rows)
         mass = jnp.sum(total[own, :], axis=1, keepdims=True)
         mixed = (acc[own, :] * (1.0 / mass)).astype(jnp.bfloat16)
-        out[:, h * vdim:(h + 1) * vdim] = jnp.dot(
-            mixed, uv[h], preferred_element_type=jnp.float32
-        ).astype(out.dtype)
+        wide_uv = jnp.concatenate([uv[first + g] for g in range(group)], axis=1)
+        both = jnp.dot(mixed, wide_uv, preferred_element_type=jnp.float32).astype(out.dtype)
+        for g in range(group):
+            out[:, (first + g) * vdim:(first + g + 1) * vdim] = both[
+                g * rows:(g + 1) * rows, g * vdim:(g + 1) * vdim
+            ]
 
     def drain(step, carry):
         for piece in range(PIECES):

time: 19.8 us -> 20 us (1.010)
  no operation moved by 1% of the time
where the time goes in v8:
time: 20 us; the launch traced here: 19.9 us
  Pallas kernels  19.2 us (96%)
  local copies, waits for them, and re-layouts  0.66 us (3%)
    pallas_call x1, Pallas kernels, body(): pl.pallas_call(functools.partial(kernel, deep, wide, heads, nope, rank),...  19.2 us
    unnamed x1, local copies, waits for them, and re-layouts  0.66 us

profile of v8, /device:TPU:25, one launch (start us, length us, event | category | flops | bytes accessed | tf_op | source)
XLA Modules:
  0.0 19.9 jit_solution(5101430451527992073)
XLA Ops:
  0.0 19.2 %shard_map.46 = bf16[16,4096]{1,0:T(8,128)(2,1)S(1)} custom-call(bf16[16,6144]{1,0:T(8,128)(2,1)} %queries.1, bf16[576,128]{1,0:T(8,128)(2,1)} %bitcast.1, bf16[32,128,512]{2,1,0:T(8,128)(2,1)} %w_uk.1, bf16[32,512,128]{2,1,0:T(8,128)(2,1)} %w_uv.1), custom_call_target="tpu_custom_call" | custom-call | tf_op jit(solution)/shard_map/pallas_call | solution.py:306
  19.2 0.7 %copy.6 = bf16[16,4096]{1,0:T(8,128)(2,1)} copy(bf16[16,4096]{1,0:T(8,128)(2,1)S(1)} %shard_map.46) | data formatting | bytes 262144

commit v9 on v7

--- a/solution.py
+++ b/solution.py
@@ -9,7 +9,7 @@
 from jax.sharding import PartitionSpec as P
 
 CORES = 2
-PIECES = 4
+PIECES = 6
 HALF = PIECES // 2
 MESH = pl.DeviceIdType.MESH
 

time: 19.8 us -> 20.2 us (1.020)
  Pallas kernels: 19 us -> 19.3 us
    pallas_call x1, Pallas kernels: 19 us -> 19.3 us  [body(): pl.pallas_call(functools.partial(kernel, deep, wide, heads, nope, rank),...]
where the time goes in v9:
time: 20.2 us; the launch traced here: 20 us
  Pallas kernels  19.3 us (96%)
  local copies, waits for them, and re-layouts  0.66 us (3%)
    pallas_call x1, Pallas kernels, body(): pl.pallas_call(functools.partial(kernel, deep, wide, heads, nope, rank),...  19.3 us
    unnamed x1, local copies, waits for them, and re-layouts  0.66 us

profile of v9, /device:TPU:25, one launch (start us, length us, event | category | flops | bytes accessed | tf_op | source)
XLA Modules:
  0.0 20.0 jit_solution(476925057226063668)
XLA Ops:
  0.0 19.3 %shard_map.46 = bf16[16,4096]{1,0:T(8,128)(2,1)S(1)} custom-call(bf16[16,6144]{1,0:T(8,128)(2,1)} %queries.1, bf16[576,128]{1,0:T(8,128)(2,1)} %bitcast.1, bf16[32,128,512]{2,1,0:T(8,128)(2,1)} %w_uk.1, bf16[32,512,128]{2,1,0:T(8,128)(2,1)} %w_uv.1), custom_call_target="tpu_custom_call" | custom-call | tf_op jit(solution)/shard_map/pallas_call | solution.py:302
  19.4 0.7 %copy.6 = bf16[16,4096]{1,0:T(8,128)(2,1)} copy(bf16[16,4096]{1,0:T(8,128)(2,1)S(1)} %shard_map.46) | data formatting | bytes 262144
